TPU v7x, 32 devices: a whole 2x2x4 slice. The times are simulated.
32 devices in a mesh: dp: 2 (over x), pipe: 2 (over core), ctx: 8 (over z, y).
Axes of the slice: x: 2, y: 2, z: 4, core: 2. Of those that a mesh axis runs over, the one named last changes fastest.
Arguments:
- section_input: bfloat16 [2, 2, 1024, 2048], P('dp', 'pipe', 'ctx'), may hold values from -6 to 6
- section_positions: int32 [2, 2, 1024], P('dp', 'pipe', 'ctx'), may hold values from 0 to 1023, as said below
- saved_input: bfloat16 [2, 2, 1024, 2048], P('dp', 'pipe', 'ctx'), may hold values from -6 to 6
- saved_positions: int32 [2, 2, 1024], P('dp', 'pipe', 'ctx'), may hold values from 0 to 1023, as said below
- cotangent: bfloat16 [2, 2, 1024, 2048], P('dp', 'pipe', 'ctx'), may hold values from -6 to 6
- norm_gains: float32 [2, 2, 2, 2048], P(None, 'pipe'), may hold values from -2 to 2
- output_gains: float32 [2, 2, 2048], P(None, 'pipe'), may hold values from 0.25 to 2
- plan: int32 [2, 2, 2], P('dp', 'pipe'), may hold values from 0 to 1
Outputs:
- next_input: bfloat16 [2, 2, 1024, 2048], P('dp', 'pipe', 'ctx')
- upstream_grad: bfloat16 [2, 2, 1024, 2048], P('dp', 'pipe', 'ctx')
- gain_grads: float32 [2, 3, 2048], P('pipe')
Inputs may be any that keep to these rules, and one draw needn't show every extreme that they name: `section_positions`: in every sequence the first position is 0 and each later one is either one more than the position before it or 0 (a new document). `saved_positions`: in every sequence the first position is 0 and each later one is either one more than the position before it or 0 (a new document).
All inputs are finite; a program needn't handle non-finite values.
Results may differ from a plain program's by a relative error of at most 0.0075.
Values may be sent and summed in bfloat16 or wider, within the bound.
A program may use at most 64 MiB of HBM per device.

v0:
```python
import jax
import jax.numpy as jnp
from jax import lax
from jax.sharding import PartitionSpec as P

HEADS = 16
HEAD_DIM = 128
FEATURES = 2048
WINDOW = 512
TOK_DEV = 128


EPSILON = 1e-06


def passed_along(value, axis, steps):
    count = lax.axis_size(axis)
    first, last = (max(0, -steps), min(count, count - steps))
    return lax.ppermute(value, axis, [(source, source + steps) for source in range(first, last)])


def shifted(value, axis, steps):
    count = lax.axis_size(axis)
    pairs = [(source, (source + steps) % count) for source in range(count)]
    return lax.ppermute(value, axis, pairs)


def as_bfloat(values):
    narrow = lax.optimization_barrier(values.astype(jnp.bfloat16)).astype(jnp.float32)
    return values + lax.stop_gradient(narrow - values)


def attend(key_rows, key_pos, key_ok, gains, query_count):
    total_rows = key_rows.shape[0]
    first_row = total_rows - query_count
    shaped = key_rows.reshape(total_rows, HEADS, HEAD_DIM)
    normed = shaped * lax.rsqrt(jnp.mean(shaped * shaped, axis=-1, keepdims=True) + EPSILON)
    query_gain = gains[0].reshape(HEADS, HEAD_DIM)
    key_gain = gains[1].reshape(HEADS, HEAD_DIM)
    queries = as_bfloat(normed[first_row:] * query_gain)
    key_vecs = as_bfloat(normed * key_gain)
    scores = jnp.einsum("qhe,khe->hqk", queries, key_vecs) / jnp.sqrt(jnp.float32(HEAD_DIM))
    query_ids = first_row + jnp.arange(query_count, dtype=jnp.int32)
    key_ids = jnp.arange(total_rows, dtype=jnp.int32)
    distance = query_ids[:, None] - key_ids[None, :]
    query_pos = key_pos[first_row:]
    allowed = (
        (distance >= 0)
        & (distance < WINDOW)
        & (query_pos[:, None] - key_pos[None, :] == distance)
        & key_ok[None, :]
    )
    weights = jnp.where(allowed[None], jnp.exp(scores), jnp.float32(0.0))
    probability = as_bfloat(weights / jnp.sum(weights, axis=-1, keepdims=True))
    mixture = jnp.einsum("hqk,khe->qhe", probability, shaped)
    return key_rows[first_row:] + mixture.reshape(query_count, FEATURES) * gains[2]


def pick_gains(norm_gains, output_gains, lap_index):
    pair_gains = lax.dynamic_index_in_dim(norm_gains, lap_index, 0, keepdims=False)[0]
    out_gain = lax.dynamic_index_in_dim(output_gains, lap_index, 0, keepdims=False)[0]
    return jnp.concatenate([pair_gains, out_gain[None]], axis=0)


def local(
    section_input,
    section_positions,
    saved_input,
    saved_positions,
    cotangent,
    norm_gains,
    output_gains,
    plan,
):
    own_rows = section_input[0, 0]
    own_pos = section_positions[0, 0]
    saved_rows = saved_input[0, 0]
    saved_pos = saved_positions[0, 0]
    incoming = cotangent[0, 0]
    shard_rows = own_rows.shape[0]
    piece_len = min(WINDOW, shard_rows)
    piece_count = WINDOW // piece_len
    shard_index = lax.axis_index("ctx")
    pieces = (own_rows, own_pos, saved_rows, saved_pos)
    received = []
    for reach in range(1, piece_count + 1):
        received.append(passed_along((pieces[0], pieces[1], pieces[2], pieces[3]), "ctx", reach))
    ordered = received[::-1]
    ok_parts = [
        jnp.broadcast_to(shard_index >= reach, (piece_len,)) for reach in range(piece_count, 0, -1)
    ]
    key_ok = jnp.concatenate(ok_parts + [jnp.ones((shard_rows,), bool)])
    forward_gains = pick_gains(norm_gains, output_gains, plan[0, 0, 0])
    backward_gains = pick_gains(norm_gains, output_gains, plan[0, 0, 1])
    forward_keys = jnp.concatenate([piece[0] for piece in ordered] + [own_rows], axis=0).astype(
        jnp.float32
    )
    forward_pos = jnp.concatenate([piece[1] for piece in ordered] + [own_pos], axis=0)
    produced = attend(forward_keys, forward_pos, key_ok, forward_gains, shard_rows).astype(
        jnp.bfloat16
    )
    next_input = shifted(produced, "pipe", 1)
    saved_keys = jnp.concatenate([piece[2] for piece in ordered] + [saved_rows], axis=0).astype(
        jnp.float32
    )
    saved_key_pos = jnp.concatenate([piece[3] for piece in ordered] + [saved_pos], axis=0)

    def local_layer(rows, gains):
        return attend(rows, saved_key_pos, key_ok, gains, shard_rows)

    _, pullback = jax.vjp(local_layer, saved_keys, backward_gains)
    key_grads, gain_grads = pullback(incoming.astype(jnp.float32))
    own_grads = key_grads[WINDOW:]
    arriving = jnp.zeros((piece_len, FEATURES), jnp.float32)
    for reach in range(1, piece_count + 1):
        first = (piece_count - reach) * piece_len
        outgoing = key_grads[first : first + piece_len].astype(jnp.bfloat16)
        arriving = arriving + passed_along(outgoing, "ctx", -reach).astype(jnp.float32)
    own_grads = own_grads.at[shard_rows - piece_len :].add(arriving)
    upstream_grad = shifted(own_grads.astype(jnp.bfloat16), "pipe", -1)
    gain_total = lax.psum(gain_grads, ("dp", "ctx"))
    gain_total = gain_total / jnp.float32(TOK_DEV)
    return (next_input[None, None], upstream_grad[None, None], gain_total[None])


def solution(mesh):
    placed = (
        P("dp", "pipe", "ctx", None),
        P("dp", "pipe", "ctx"),
        P("dp", "pipe", "ctx", None),
        P("dp", "pipe", "ctx"),
        P("dp", "pipe", "ctx", None),
        P(None, "pipe", None, None),
        P(None, "pipe", None),
        P("dp", "pipe", None),
    )
    return jax.shard_map(
        local,
        mesh=mesh,
        in_specs=placed,
        out_specs=(
            P("dp", "pipe", "ctx", None),
            P("dp", "pipe", "ctx", None),
            P("pipe", None, None),
        ),
        check_vma=False,
    )
```

profile of v0, /device:TPU:0, one launch (start us, length us, event | category | flops | bytes accessed | tf_op | source)
XLA Modules:
  0.0 320.6 jit_solution(6539457708362573059)
XLA Ops:
  0.6 6.0 %collective-permute-start.13 = (bf16[128,2048]{1,0:T(8,128)(2,1)}, bf16[128,2048]{1,0:T(8,128)(2,1)S(1)}, u32[]{:S(2)}, u32[]{:S(2)}) collective-permute-start(bf16[128,2048]{1,0:T(8,128)(2,1)} %bitcast.86), channel_id=1, source_target_pairs={{0,4},{1,5},{2,6},{3,7},{8,12},{9,13},{10,14},{11,15},{16,20},{17,... | collective-permute-start | bytes 1572872 | tf_op jit(solution)/shard_map/ppermute | solution.py:19
  6.6 4.5 %collective-permute-start.14 = (bf16[128,2048]{1,0:T(8,128)(2,1)}, bf16[128,2048]{1,0:T(8,128)(2,1)S(1)}, u32[]{:S(2)}, u32[]{:S(2)}) collective-permute-start(bf16[128,2048]{1,0:T(8,128)(2,1)} %bitcast.87), channel_id=1, source_target_pairs={{0,3},{1,4},{2,5},{3,6},{4,7},{8,11},{9,12},{10,13},{11,14},{12,15... | collective-permute-start | bytes 1572872 | tf_op jit(solution)/shard_map/ppermute | solution.py:19
  12.4 3.9 %collective-permute-start.16 = (bf16[128,2048]{1,0:T(8,128)(2,1)}, bf16[128,2048]{1,0:T(8,128)(2,1)}, u32[]{:S(2)}, u32[]{:S(2)}) collective-permute-start(bf16[128,2048]{1,0:T(8,128)(2,1)} %bitcast.89), channel_id=1, source_target_pairs={{0,1},{1,2},{2,3},{3,4},{4,5},{5,6},{6,7},{8,9},{9,10},{10,11},{11... | collective-permute-start | bytes 1572872 | tf_op jit(solution)/shard_map/ppermute | solution.py:19
  32.2 8.4 %collective-permute-done.4 = s32[128]{0:T(128)S(1)} collective-permute-done((s32[128]{0:T(128)}, s32[128]{0:T(128)S(1)}, u32[]{:S(2)}, u32[]{:S(2)}) %collective-permute-start.4) | collective-permute-done | bytes 544 | tf_op jit(solution)/shard_map/ppermute | solution.py:19
  40.6 38.0 %collective-permute-start.5 = (s32[128]{0:T(128)}, s32[128]{0:T(128)S(1)}, u32[]{:S(2)}, u32[]{:S(2)}) collective-permute-start(s32[128]{0:T(128)} %bitcast.117), channel_id=1, source_target_pairs={{0,3},{1,4},{2,5},{3,6},{4,7},{8,11},{9,12},{10,13},{11,14},{12,15... | collective-permute-start | bytes 1544 | tf_op jit(solution)/shard_map/ppermute | solution.py:19
  82.7 6.2 %collective-permute-start.7 = (s32[128]{0:T(128)}, s32[128]{0:T(128)S(1)}, u32[]{:S(2)}, u32[]{:S(2)}) collective-permute-start(s32[128]{0:T(128)} %bitcast.119), channel_id=1, source_target_pairs={{0,1},{1,2},{2,3},{3,4},{4,5},{5,6},{6,7},{8,9},{9,10},{10,11},{11... | collective-permute-start | bytes 1544 | tf_op jit(solution)/shard_map/ppermute | solution.py:19
  90.4 6.8 %collective-permute-start.9 = (s32[128]{0:T(128)}, s32[128]{0:T(128)S(1)}, u32[]{:S(2)}, u32[]{:S(2)}) collective-permute-start(s32[128]{0:T(128)} %bitcast.111), channel_id=1, source_target_pairs={{0,4},{1,5},{2,6},{3,7},{8,12},{9,13},{10,14},{11,15},{16,20},{17,... | collective-permute-start | bytes 1544 | tf_op jit(solution)/shard_map/ppermute | solution.py:19
  98.6 4.1 %collective-permute-start.10 = (s32[128]{0:T(128)}, s32[128]{0:T(128)S(1)}, u32[]{:S(2)}, u32[]{:S(2)}) collective-permute-start(s32[128]{0:T(128)} %bitcast.112), channel_id=1, source_target_pairs={{0,3},{1,4},{2,5},{3,6},{4,7},{8,11},{9,12},{10,13},{11,14},{12,15... | collective-permute-start | bytes 1544 | tf_op jit(solution)/shard_map/ppermute | solution.py:19
  104.2 3.4 %collective-permute-start.11 = (s32[128]{0:T(128)}, s32[128]{0:T(128)S(1)}, u32[]{:S(2)}, u32[]{:S(2)}) collective-permute-start(s32[128]{0:T(128)} %bitcast.113), channel_id=1, source_target_pairs={{0,2},{1,3},{2,4},{3,5},{4,6},{5,7},{8,10},{9,11},{10,12},{11,13},... | collective-permute-start | bytes 1544 | tf_op jit(solution)/shard_map/ppermute | solution.py:19
  109.0 4.1 %collective-permute-start.12 = (s32[128]{0:T(128)}, s32[128]{0:T(128)S(1)}, u32[]{:S(2)}, u32[]{:S(2)}) collective-permute-start(s32[128]{0:T(128)} %bitcast.114), channel_id=1, source_target_pairs={{0,1},{1,2},{2,3},{3,4},{4,5},{5,6},{6,7},{8,9},{9,10},{10,11},{11... | collective-permute-start | bytes 1544 | tf_op jit(solution)/shard_map/ppermute | solution.py:19
  114.5 19.6 %collective-permute-start = (bf16[128,2048]{1,0:T(8,128)(2,1)}, bf16[128,2048]{1,0:T(8,128)(2,1)}, u32[]{:S(2)}, u32[]{:S(2)}) collective-permute-start(bf16[128,2048]{1,0:T(8,128)(2,1)} %bitcast), channel_id=1, source_target_pairs={{0,4},{1,5},{2,6},{3,7},{8,12},{9,13},{10,14},{11,15},{16,20},{17,... | collective-permute-start | bytes 1572872 | tf_op jit(solution)/shard_map/ppermute | solution.py:19
  142.0 3.3 %collective-permute-start.3 = (bf16[128,2048]{1,0:T(8,128)(2,1)}, bf16[128,2048]{1,0:T(8,128)(2,1)}, u32[]{:S(2)}, u32[]{:S(2)}) collective-permute-start(bf16[128,2048]{1,0:T(8,128)(2,1)} %bitcast), channel_id=1, source_target_pairs={{0,1},{1,2},{2,3},{3,4},{4,5},{5,6},{6,7},{8,9},{9,10},{10,11},{11... | collective-permute-start | bytes 1572872 | tf_op jit(solution)/shard_map/ppermute | solution.py:19
  156.0 2.7 fusion.14
  158.8 4.1 %fusion.59 = (bf16[16,128,640]{2,1,0:T(8,128)(2,1)}, f32[16,128]{1,0:T(8,128)S(1)}, f32[16,128,640]{2,1,0:T(8,128)S(1)}) fusion(f32[16,128]{1,0:T(8,128)S(1)} %get-tuple-element.51, f32[16,128,640]{2,1,0:T(8,128)S(1)} %get-tuple-element.52, pred[128,640]{1,0:T(8,128)(4,1)S(1)} %get-tuple-element.45, f32[16,128]{1,0:T(8,128)S(1)} %multiply_divide_fusion, ...), kind=kOutput, calls=%fused_computation.121 | convolution fusion | flops 345241600 | bytes 16367616 | tf_op jit(solution)/shard_map/transpose(jvp(hqk,khe->qhe))/dot_general | solution.py:55
  162.9 3.4 %multiply_reduce_fusion.1 = (f32[16,128]{1,0:T(8,128)S(1)}, f32[128,16,128]{0,2,1:T(8,128)S(1)}) fusion(f32[640,16,128]{0,2,1:T(8,128)S(1)} %get-tuple-element.29, f32[16,128]{1,0:T(8,128)S(1)} %bitcast.104, bf16[640,16,128]{0,2,1:T(8,128)(2,1)S(1)} %get-tuple-element.30, bf16[640,16,128]{0,2,1:T(8,128)(2,1)S(1)} %constant_dynamic-update-slice_fusion.7, ...), kind=kOutput, calls=%fused_computation.58 | convolution fusion | flops 352057344 | bytes 17989632 | tf_op jit(solution)/shard_map/transpose(jvp(qhe,khe->hqk))/dot_general | solution.py:42
  166.3 3.9 %fusion.6 = (f32[16,128]{1,0:T(8,128)S(1)}, f32[640,16]{0,1:T(8,128)S(1)}, f32[16,640,128]{1,2,0:T(8,128)S(1)}) fusion(bf16[640,16,128]{0,2,1:T(8,128)(2,1)S(1)} %constant_dynamic-update-slice_fusion.7, f32[640,16]{0,1:T(8,128)S(1)} %fusion.54, f32[128,16,128]{0,2,1:T(8,128)S(1)} %get-tuple-element.38, f32[16,128]{1,0:T(8,128)S(1)} %bitcast.100, ...), kind=kOutput, calls=%fused_computation.19 | convolution fusion | flops 354930688 | bytes 21176320 | tf_op jit(solution)/shard_map/transpose(jvp(qhe,khe->hqk))/dot_general | solution.py:42
  170.3 4.0 %fusion.27 = f32[16,128]{1,0:T(8,128)S(1)} fusion(f32[128,16,128]{2,0,1:T(8,128)S(1)} %copy-done.2, bf16[640,16,128]{0,2,1:T(8,128)(2,1)S(1)} %constant_dynamic-update-slice_fusion.7, bf16[16,128,640]{2,1,0:T(8,128)(2,1)} %get-tuple-element.27, f32[16,128,640]{2,1,0:T(8,128)S(1)} %get-tuple-element.52, f32[16,128]{1,0:T(8,128)S(1)} %get-tuple-element.51, ...), kind=kOutput, calls=%fused_computation.50 | convolution fusion | flops 343930880 | bytes 11632640 | tf_op jit(solution)/shard_map/jvp(hqk,khe->qhe)/dot_general | solution.py:55
  174.3 4.9 %add_add_fusion = f32[640,16,128]{0,2,1:T(8,128)} fusion(bf16[640,16,128]{0,2,1:T(8,128)(2,1)S(1)} %constant_dynamic-update-slice_fusion.7, f32[128,16,128]{0,2,1:T(8,128)S(1)} %get-tuple-element.38, f32[16,640,128]{1,2,0:T(8,128)S(1)} %get-tuple-element.54, f32[640,16]{0,1:T(8,128)S(1)} %multiply_multiply_fusion.1, f32[16,128]{1,0:T(8,128)S(1)} %bitcast.101, ...), kind=kOutput, calls=%fused_computation.4 | convolution fusion | flops 354418688 | bytes 22732800 | tf_op jit(solution)/shard_map/transpose(jvp(hqk,khe->qhe))/dot_general | solution.py:55
  179.2 6.0 %copy.48 = f32[640,2048]{1,0:T(8,128)} copy(f32[640,2048]{0,1:T(8,128)} %bitcast.70) | data formatting | bytes 10485760 | tf_op jit(solution)/shard_map/transpose(jvp())/reshape | solution.py:36
  185.1 6.1 %fusion.60 = (bf16[640,2048]{1,0:T(8,128)(2,1)S(1)}, f32[640,2048]{1,0:T(8,128)}) fusion(f32[640,2048]{1,0:T(8,128)} %copy.48, bf16[128,2048]{1,0:T(8,128)(2,1)S(1)} %bitcast.84), kind=kLoop, calls=%fused_computation.122 | loop fusion | flops 3932160 | bytes 13631488 | tf_op jit(solution)/shard_map/convert.8
  212.9 2.8 fusion.12
  216.8 3.3 %fusion.2 = f32[16,128,128]{2,1,0:T(8,128)} fusion(bf16[640,16,128]{0,2,1:T(8,128)(2,1)S(1)} %constant_dynamic-update-slice_fusion, bf16[16,128,640]{2,1,0:T(8,128)(2,1)S(1)} %fusion.29, f32[16,128,640]{2,1,0:T(8,128)S(1)} %get-tuple-element.50, f32[16,128]{1,0:T(8,128)S(1)} %get-tuple-element.49, pred[128,640]{1,0:T(8,128)(4,1)S(1)} %get-tuple-element.46), kind=kOutput, calls=%fused_computation.13 | convolution fusion | flops 343408640 | bytes 11624448 | tf_op jit(solution)/shard_map/hqk,khe->qhe/dot_general | solution.py:55
  223.0 21.3 %collective-permute-done.20 = bf16[128,2048]{1,0:T(8,128)(2,1)} collective-permute-done((bf16[128,2048]{1,0:T(8,128)(2,1)}, bf16[128,2048]{1,0:T(8,128)(2,1)}, u32[]{:S(2)}, u32[]{:S(2)}) %collective-permute-start.20) | collective-permute-done | bytes 524320 | tf_op jit(solution)/shard_map/ppermute | solution.py:19
  246.6 71.7 %psum.7 = f32[3,2048]{1,0:T(4,128)S(1)} all-reduce(f32[3,2048]{1,0:T(4,128)S(1)} %pad_add_fusion), channel_id=1, replica_groups=mesh['dp'=2,'pipe'=2,'ctx'=8] {'dp','ctx'}, use_global_device_ids=true, to_apply=%region_9.10 | all-reduce | flops 6144 | bytes 49152 | tf_op jit(solution)/shard_map/psum | solution.py:121
  (110 shorter events, 73.0 us)
Async XLA Ops:
  0.6 135.2 %collective-permute-start.13 = (bf16[128,2048]{1,0:T(8,128)(2,1)}, bf16[128,2048]{1,0:T(8,128)(2,1)S(1)}, u32[]{:S(2)}, u32[]{:S(2)}) collective-permute-start(bf16[128,2048]{1,0:T(8,128)(2,1)} %bitcast.86), channel_id=1, source_target_pairs={{0,4},{1,5},{2,6},{3,7},{8,12},{9,13},{10,14},{11,15},{16,20},{17,... | collective-permute-start | bytes 1572872 | tf_op jit(solution)/shard_map/ppermute | solution.py:19
  6.6 132.3 %collective-permute-start.14 = (bf16[128,2048]{1,0:T(8,128)(2,1)}, bf16[128,2048]{1,0:T(8,128)(2,1)S(1)}, u32[]{:S(2)}, u32[]{:S(2)}) collective-permute-start(bf16[128,2048]{1,0:T(8,128)(2,1)} %bitcast.87), channel_id=1, source_target_pairs={{0,3},{1,4},{2,5},{3,6},{4,7},{8,11},{9,12},{10,13},{11,14},{12,15... | collective-permute-start | bytes 1572872 | tf_op jit(solution)/shard_map/ppermute | solution.py:19
  11.1 130.9 %collective-permute-start.15 = (bf16[128,2048]{1,0:T(8,128)(2,1)}, bf16[128,2048]{1,0:T(8,128)(2,1)S(1)}, u32[]{:S(2)}, u32[]{:S(2)}) collective-permute-start(bf16[128,2048]{1,0:T(8,128)(2,1)} %bitcast.88), channel_id=1, source_target_pairs={{0,2},{1,3},{2,4},{3,5},{4,6},{5,7},{8,10},{9,11},{10,12},{11,13},... | collective-permute-start | bytes 1572872 | tf_op jit(solution)/shard_map/ppermute | solution.py:19
  12.4 137.4 %collective-permute-start.16 = (bf16[128,2048]{1,0:T(8,128)(2,1)}, bf16[128,2048]{1,0:T(8,128)(2,1)}, u32[]{:S(2)}, u32[]{:S(2)}) collective-permute-start(bf16[128,2048]{1,0:T(8,128)(2,1)} %bitcast.89), channel_id=1, source_target_pairs={{0,1},{1,2},{2,3},{3,4},{4,5},{5,6},{6,7},{8,9},{9,10},{10,11},{11... | collective-permute-start | bytes 1572872 | tf_op jit(solution)/shard_map/ppermute | solution.py:19
  16.3 24.3 %collective-permute-start.4 = (s32[128]{0:T(128)}, s32[128]{0:T(128)S(1)}, u32[]{:S(2)}, u32[]{:S(2)}) collective-permute-start(s32[128]{0:T(128)} %bitcast.116), channel_id=1, source_target_pairs={{0,4},{1,5},{2,6},{3,7},{8,12},{9,13},{10,14},{11,15},{16,20},{17,... | collective-permute-start | bytes 1544 | tf_op jit(solution)/shard_map/ppermute | solution.py:19
  40.6 39.4 %collective-permute-start.5 = (s32[128]{0:T(128)}, s32[128]{0:T(128)S(1)}, u32[]{:S(2)}, u32[]{:S(2)}) collective-permute-start(s32[128]{0:T(128)} %bitcast.117), channel_id=1, source_target_pairs={{0,3},{1,4},{2,5},{3,6},{4,7},{8,11},{9,12},{10,13},{11,14},{12,15... | collective-permute-start | bytes 1544 | tf_op jit(solution)/shard_map/ppermute | solution.py:19
  80.0 2.7 collective-permute-start.6
  82.7 7.6 %collective-permute-start.7 = (s32[128]{0:T(128)}, s32[128]{0:T(128)S(1)}, u32[]{:S(2)}, u32[]{:S(2)}) collective-permute-start(s32[128]{0:T(128)} %bitcast.119), channel_id=1, source_target_pairs={{0,1},{1,2},{2,3},{3,4},{4,5},{5,6},{6,7},{8,9},{9,10},{10,11},{11... | collective-permute-start | bytes 1544 | tf_op jit(solution)/shard_map/ppermute | solution.py:19
  90.4 8.2 %collective-permute-start.9 = (s32[128]{0:T(128)}, s32[128]{0:T(128)S(1)}, u32[]{:S(2)}, u32[]{:S(2)}) collective-permute-start(s32[128]{0:T(128)} %bitcast.111), channel_id=1, source_target_pairs={{0,4},{1,5},{2,6},{3,7},{8,12},{9,13},{10,14},{11,15},{16,20},{17,... | collective-permute-start | bytes 1544 | tf_op jit(solution)/shard_map/ppermute | solution.py:19
  98.6 5.6 %collective-permute-start.10 = (s32[128]{0:T(128)}, s32[128]{0:T(128)S(1)}, u32[]{:S(2)}, u32[]{:S(2)}) collective-permute-start(s32[128]{0:T(128)} %bitcast.112), channel_id=1, source_target_pairs={{0,3},{1,4},{2,5},{3,6},{4,7},{8,11},{9,12},{10,13},{11,14},{12,15... | collective-permute-start | bytes 1544 | tf_op jit(solution)/shard_map/ppermute | solution.py:19
  104.2 4.8 %collective-permute-start.11 = (s32[128]{0:T(128)}, s32[128]{0:T(128)S(1)}, u32[]{:S(2)}, u32[]{:S(2)}) collective-permute-start(s32[128]{0:T(128)} %bitcast.113), channel_id=1, source_target_pairs={{0,2},{1,3},{2,4},{3,5},{4,6},{5,7},{8,10},{9,11},{10,12},{11,13},... | collective-permute-start | bytes 1544 | tf_op jit(solution)/shard_map/ppermute | solution.py:19
  109.0 5.6 %collective-permute-start.12 = (s32[128]{0:T(128)}, s32[128]{0:T(128)S(1)}, u32[]{:S(2)}, u32[]{:S(2)}) collective-permute-start(s32[128]{0:T(128)} %bitcast.114), channel_id=1, source_target_pairs={{0,1},{1,2},{2,3},{3,4},{4,5},{5,6},{6,7},{8,9},{9,10},{10,11},{11... | collective-permute-start | bytes 1544 | tf_op jit(solution)/shard_map/ppermute | solution.py:19
  114.5 79.5 %collective-permute-start = (bf16[128,2048]{1,0:T(8,128)(2,1)}, bf16[128,2048]{1,0:T(8,128)(2,1)}, u32[]{:S(2)}, u32[]{:S(2)}) collective-permute-start(bf16[128,2048]{1,0:T(8,128)(2,1)} %bitcast), channel_id=1, source_target_pairs={{0,4},{1,5},{2,6},{3,7},{8,12},{9,13},{10,14},{11,15},{16,20},{17,... | collective-permute-start | bytes 1572872 | tf_op jit(solution)/shard_map/ppermute | solution.py:19
  135.8 61.6 %collective-permute-start.1 = (bf16[128,2048]{1,0:T(8,128)(2,1)}, bf16[128,2048]{1,0:T(8,128)(2,1)}, u32[]{:S(2)}, u32[]{:S(2)}) collective-permute-start(bf16[128,2048]{1,0:T(8,128)(2,1)} %bitcast), channel_id=1, source_target_pairs={{0,3},{1,4},{2,5},{3,6},{4,7},{8,11},{9,12},{10,13},{11,14},{12,15... | collective-permute-start | bytes 1572872 | tf_op jit(solution)/shard_map/ppermute | solution.py:19
  138.9 62.1 %collective-permute-start.2 = (bf16[128,2048]{1,0:T(8,128)(2,1)}, bf16[128,2048]{1,0:T(8,128)(2,1)}, u32[]{:S(2)}, u32[]{:S(2)}) collective-permute-start(bf16[128,2048]{1,0:T(8,128)(2,1)} %bitcast), channel_id=1, source_target_pairs={{0,2},{1,3},{2,4},{3,5},{4,6},{5,7},{8,10},{9,11},{10,12},{11,13},... | collective-permute-start | bytes 1572872 | tf_op jit(solution)/shard_map/ppermute | solution.py:19
  142.0 65.8 %collective-permute-start.3 = (bf16[128,2048]{1,0:T(8,128)(2,1)}, bf16[128,2048]{1,0:T(8,128)(2,1)}, u32[]{:S(2)}, u32[]{:S(2)}) collective-permute-start(bf16[128,2048]{1,0:T(8,128)(2,1)} %bitcast), channel_id=1, source_target_pairs={{0,1},{1,2},{2,3},{3,4},{4,5},{5,6},{6,7},{8,9},{9,10},{10,11},{11... | collective-permute-start | bytes 1572872 | tf_op jit(solution)/shard_map/ppermute | solution.py:19
  179.2 6.0 %copy-start.1 = (bf16[1,1,128,2048]{3,2,1,0:T(8,128)(2,1)S(1)}, bf16[1,1,128,2048]{3,2,1,0:T(8,128)(2,1)}, u32[]{:S(2)}) copy-start(bf16[1,1,128,2048]{3,2,1,0:T(8,128)(2,1)} %param.16) | copy-start | bytes 1572868
  192.6 18.4 %copy-start = (bf16[1,1,128,2048]{2,3,1,0:T(8,128)(2,1)S(1)}, bf16[1,1,128,2048]{2,3,1,0:T(8,128)(2,1)}, u32[]{:S(2)}) copy-start(bf16[1,1,128,2048]{2,3,1,0:T(8,128)(2,1)} %copy.34) | copy-start | bytes 1572868
  192.6 30.3 %collective-permute-start.17 = (bf16[128,2048]{1,0:T(8,128)(2,1)}, bf16[128,2048]{1,0:T(8,128)(2,1)}, u32[]{:S(2)}, u32[]{:S(2)}) collective-permute-start(bf16[128,2048]{1,0:T(8,128)(2,1)} %get-tuple-element.33), channel_id=1, source_target_pairs={{1,0},{2,1},{3,2},{4,3},{5,4},{6,5},{7,6},{9,8},{10,9},{11,10},{12... | collective-permute-start | bytes 1572872 | tf_op jit(solution)/shard_map/ppermute | solution.py:19
  194.1 28.9 %collective-permute-start.18 = (bf16[128,2048]{1,0:T(8,128)(2,1)}, bf16[128,2048]{1,0:T(8,128)(2,1)}, u32[]{:S(2)}, u32[]{:S(2)}) collective-permute-start(bf16[128,2048]{1,0:T(8,128)(2,1)} %get-tuple-element.36), channel_id=1, source_target_pairs={{2,0},{3,1},{4,2},{5,3},{6,4},{7,5},{10,8},{11,9},{12,10},{13,11},... | collective-permute-start | bytes 1572872 | tf_op jit(solution)/shard_map/ppermute | solution.py:19
  197.4 25.6 %collective-permute-start.19 = (bf16[128,2048]{1,0:T(8,128)(2,1)}, bf16[128,2048]{1,0:T(8,128)(2,1)}, u32[]{:S(2)}, u32[]{:S(2)}) collective-permute-start(bf16[128,2048]{1,0:T(8,128)(2,1)} %get-tuple-element.35), channel_id=1, source_target_pairs={{3,0},{4,1},{5,2},{6,3},{7,4},{11,8},{12,9},{13,10},{14,11},{15,12... | collective-permute-start | bytes 1572872 | tf_op jit(solution)/shard_map/ppermute | solution.py:19
  201.0 43.3 %collective-permute-start.20 = (bf16[128,2048]{1,0:T(8,128)(2,1)}, bf16[128,2048]{1,0:T(8,128)(2,1)}, u32[]{:S(2)}, u32[]{:S(2)}) collective-permute-start(bf16[128,2048]{1,0:T(8,128)(2,1)} %get-tuple-element.34), channel_id=1, source_target_pairs={{4,0},{5,1},{6,2},{7,3},{12,8},{13,9},{14,10},{15,11},{20,16},{21,... | collective-permute-start | bytes 1572872 | tf_op jit(solution)/shard_map/ppermute | solution.py:19
  222.9 96.1 %collective-permute-start.8 = (bf16[128,2048]{1,0:T(8,128)(2,1)S(1)}, bf16[128,2048]{1,0:T(8,128)(2,1)S(1)}, u32[]{:S(2)}, u32[]{:S(2)}) collective-permute-start(bf16[128,2048]{1,0:T(8,128)(2,1)S(1)} %add_convert_fusion), channel_id=1, source_target_pairs={{0,8},{8,0},{1,9},{9,1},{2,10},{10,2},{3,11},{11,3},{4,12},{12,4},... | collective-permute-start | bytes 1572872 | tf_op jit(solution)/shard_map/ppermute | solution.py:25
  246.5 72.5 %collective-permute-start.21 = (bf16[128,2048]{1,0:T(8,128)(2,1)S(1)}, bf16[128,2048]{1,0:T(8,128)(2,1)S(1)}, u32[]{:S(2)}, u32[]{:S(2)}) collective-permute-start(bf16[128,2048]{1,0:T(8,128)(2,1)S(1)} %fusion.30), channel_id=1, source_target_pairs={{0,8},{8,0},{1,9},{9,1},{2,10},{10,2},{3,11},{11,3},{4,12},{12,4},... | collective-permute-start | bytes 1572872 | tf_op jit(solution)/shard_map/ppermute | solution.py:25
  (2 other events, 7.9 us)
where the time goes:
time: 322 us; the launch traced here: 321 us
  starting transfers between devices  114 us (35%)
  blocking collectives  71.7 us (22%)
  local copies, waits for them, and re-layouts  47.1 us (15%)
  waiting for transfers between devices  38.8 us (12%)
  matrix products  29.1 us (9%)
  other arithmetic  15.1 us (5%)
  between operations  5.06 us (2%)
    ppermute x20, starting transfers between devices, passed_along(): lax.ppermute(value, axis, [(source, source + steps) for source in range(f...  113 us
    psum x1, blocking collectives, local(): gain_total = lax.psum(gain_grads, ('dp', 'ctx'))  71.7 us
    ppermute x20, waiting for transfers between devices, passed_along(): lax.ppermute(value, axis, [(source, source + steps) for source in range(f...  38.8 us
    unnamed x33, local copies, waits for them, and re-layouts  17.3 us
    dot_general x4, matrix products, attend(): mixture = jnp.einsum('hqk,khe->qhe', probability, shaped)  16.3 us
    ppermute x8, local copies, waits for them, and re-layouts, passed_along(): lax.ppermute(value, axis, [(source, source + steps) for source in range(f...  13.2 us
    dot_general x4, matrix products, attend(): jnp.einsum('qhe,khe->hqk', queries, key_vecs)  12.8 us
  transfers between devices with their start and end apart: 22, of which 9 were waited for; matrix products, arithmetic and copies ran while one was open for 28% of the time, Pallas kernels for 0%

commit v1 on v0

v1 whole, which is shorter than its diff:
```python
import functools

import jax
import jax.numpy as jnp
from jax import lax
from jax.experimental import pallas as pl
from jax.experimental.pallas import tpu as pltpu
from jax.sharding import PartitionSpec as P

HEADS = 16
HEAD_DIM = 128
FEATURES = 2048
WINDOW = 512
TOK = 128
REACH = WINDOW // TOK
SPAN = WINDOW + TOK
CHUNKS = 4
WIDTH = FEATURES // CHUNKS
CHUNK_HEADS = HEADS // CHUNKS
EPSILON = 1e-06
SCALE = HEAD_DIM**-0.5
MESH = pl.DeviceIdType.MESH
F32 = jnp.float32
BF16 = jnp.bfloat16
A, B, C, D = range(4)


def sum_stages(sizes):
    stages = []
    for axis in ("dp", "ctx"):
        left, stride = sizes[axis], 1
        while left > 1:
            factor = next(f for f in range(2, left + 1) if left % f == 0)
            stages.append((axis, stride, factor))
            left //= factor
            stride *= factor
    return stages


def slot(reach):
    return (REACH - reach) * TOK


def dot(left, right, left_dim, right_dim):
    return lax.dot_general(
        left, right, (((left_dim,), (right_dim,)), ((), ())), preferred_element_type=F32
    )


def kernel(
    sizes,
    sec_ref,
    sec_pos,
    sav_ref,
    sav_pos,
    cot_ref,
    norm_ref,
    outg_ref,
    plan_ref,
    next_ref,
    up_ref,
    total_ref,
    keys,
    cot,
    gains,
    masks,
    grads,
    own,
    from_partner,
    from_z4,
    from_z2,
    produced,
    dx,
    sums,
    load_sem,
    key_send,
    key_recv,
    grad_send,
    grad_recv,
    out_send,
    out_recv,
    sum_send,
    sum_recv,
):
    n = sizes["ctx"]
    c = lax.axis_index("ctx")
    odd = lax.rem(c, 2)
    even = odd == 0
    partner = c + 1 - 2 * odd
    pipe = lax.axis_index("pipe")
    after = lax.rem(pipe + 1, sizes["pipe"])
    before = lax.rem(pipe + sizes["pipe"] - 1, sizes["pipe"])
    up, down = c + 2 < n, c >= 2
    stages = sum_stages(sizes)

    def rows(first):
        if isinstance(first, int):
            return pl.ds(first, TOK)
        return pl.ds(pl.multiple_of(first, TOK), TOK)

    def columns(j):
        return pl.ds(pl.multiple_of(j * WIDTH, WIDTH), WIDTH)

    def load(which, j):
        source = (sav_ref, sec_ref, cot_ref)[which]
        target = cot.at[j] if which == 2 else keys.at[which, j, rows(WINDOW)]
        return pltpu.make_async_copy(source.at[:, columns(j)], target, load_sem.at[which, j])

    def key_copy(t, kind, j):
        if kind == A:
            source, target, device = slot(0), slot(2), c + 2
        elif kind == B:
            source, target, device = slot(2), slot(4), c + 2
        elif kind == C:
            source, target, device = jnp.where(even, slot(0), slot(2)), slot(1), partner
        else:
            source, target, device = jnp.where(even, slot(2), slot(4)), slot(3), partner
        return pltpu.make_async_remote_copy(
            src_ref=keys.at[t, j, rows(source)],
            dst_ref=keys.at[t, j, rows(target)],
            send_sem=key_send.at[t, kind, j],
            recv_sem=key_recv.at[t, kind, j],
            device_id={"ctx": device},
            device_id_type=MESH,
        )

    sends_key = (up, up & down, even | down, c >= 2 + 2 * odd)
    gets_key = (c >= 2, c >= 4, c >= 1, c >= 3)

    def grad_copy(kind, j):
        if kind < 2:
            source, target, device = slot((1, 3)[kind]), from_partner.at[kind, j], partner
        else:
            source, target, device = slot((4, 2)[kind - 2]), (from_z4, from_z2)[kind - 2].at[j], c - 2
        return pltpu.make_async_remote_copy(
            src_ref=grads.at[j, rows(source)],
            dst_ref=target,
            send_sem=grad_send.at[kind, j],
            recv_sem=grad_recv.at[kind, j],
            device_id={"ctx": device},
            device_id_type=MESH,
        )

    sends_grad = (None, None, c >= 4, down)
    gets_grad = (None, None, down & up, up)

    def out_copy(kind, j):
        return pltpu.make_async_remote_copy(
            src_ref=(produced, dx)[kind].at[j],
            dst_ref=(next_ref, up_ref)[kind].at[:, columns(j)],
            send_sem=out_send.at[kind, j],
            recv_sem=out_recv.at[kind, j],
            device_id={"pipe": (after, before)[kind]},
            device_id_type=MESH,
        )

    def digit_of(stage):
        axis, stride, factor = stages[stage]
        return lax.rem(lax.axis_index(axis) // stride, factor)

    def sum_peer(stage, offset):
        axis, stride, factor = stages[stage]
        digit = digit_of(stage)
        return {axis: lax.axis_index(axis) + (lax.rem(digit + offset, factor) - digit) * stride}

    def sum_copy(stage, offset, sender):
        return pltpu.make_async_remote_copy(
            src_ref=sums.at[stage, digit_of(stage)],
            dst_ref=sums.at[stage, sender],
            send_sem=sum_send.at[stage, offset - 1],
            recv_sem=sum_recv.at[stage, offset - 1],
            device_id=sum_peer(stage, offset),
            device_id_type=MESH,
        )

    def start_sum(stage):
        for offset in range(1, stages[stage][2]):
            sum_copy(stage, offset, digit_of(stage)).start()

    def finish_sum(stage):
        factor = stages[stage][2]
        for offset in range(1, factor):
            sender = lax.rem(digit_of(stage) + factor - offset, factor)
            sum_copy(stage, offset, sender).wait_recv()
        total = sums[stage, 0]
        for digit in range(1, factor):
            total = total + sums[stage, digit]
        if stage + 1 < len(stages):
            sums[stage + 1, digit_of(stage + 1)] = total
            start_sum(stage + 1)
        else:
            total_ref[...] = total * (1.0 / TOK)

    def when(condition, action):
        if condition is None:
            action()
        else:
            pl.when(condition)(action)

    def start_key(t, kind, j, extra=None):
        condition = sends_key[kind]
        if extra is not None:
            condition = condition & extra
        when(condition, lambda: key_copy(t, kind, j).start())

    def wait_key(t, kind, j):
        when(gets_key[kind], lambda: key_copy(t, kind, j).wait_recv())

    def each(action):
        @pl.loop(0, CHUNKS)
        def _(j):
            action(j)

    each(lambda j: load(0, j).start())
    barrier = pltpu.get_barrier_semaphore()

    def greet(device):
        pl.semaphore_signal(barrier, inc=1, device_id=device, device_id_type=MESH)

    greet({"ctx": partner})
    greet({"pipe": after})
    count = 2
    if sizes["pipe"] > 2:
        greet({"pipe": before})
        count += 1
    pl.when(up)(lambda: greet({"ctx": c + 2}))
    pl.when(down)(lambda: greet({"ctx": c - 2}))
    for stage, (axis, stride, factor) in enumerate(stages):
        if axis == "ctx" and factor == 2 and stride <= 2:
            continue
        for offset in range(1, factor):
            greet(sum_peer(stage, offset))
            count += 1
    each(lambda j: load(1, j).start())
    each(lambda j: load(2, j).start())
    pl.semaphore_wait(barrier, count + up.astype(jnp.int32) + down.astype(jnp.int32))

    def first_saved(j):
        load(0, j).wait()
        start_key(0, A, j)
        start_key(0, C, j, even)

    each(first_saved)

    for which in range(2):
        lap = plan_ref[0, which]
        gains[pl.ds(3 * which, 2), :] = jnp.where(lap == 1, norm_ref[1], norm_ref[0])
        gains[pl.ds(3 * which + 2, 1), :] = jnp.where(lap == 1, outg_ref[1], outg_ref[0])
    distance = (
        lax.broadcasted_iota(jnp.int32, (SPAN, TOK), 1)
        + WINDOW
        - lax.broadcasted_iota(jnp.int32, (SPAN, TOK), 0)
    )
    for t, positions in ((0, sav_pos), (1, sec_pos)):
        allowed = (distance >= 0) & (distance < WINDOW) & (distance <= positions[...])
        masks[t] = jnp.where(allowed, 1.0, 0.0).astype(F32)
    for reach in range(1, REACH + 1):

        @pl.when(c < reach)
        def _():
            @pl.loop(0, CHUNKS)
            def _(j):
                for t in range(2):
                    keys[t, j, rows(slot(reach))] = jnp.zeros((TOK, WIDTH), BF16)

    def relay(t, j):
        wait_key(t, A, j)
        start_key(t, B, j)
        start_key(t, C, j, odd == 1)
        start_key(t, D, j, even)

    def relay_last(t, j):
        wait_key(t, B, j)
        start_key(t, D, j, odd == 1)

    each(lambda j: relay(0, j))

    def second(j):
        relay_last(0, j)
        load(1, j).wait()
        start_key(1, A, j)
        start_key(1, C, j, even)

    each(second)

    def normed(x):
        wide = x.astype(F32)
        inverse = lax.rsqrt(jnp.mean(wide * wide, axis=-1, keepdims=True) + EPSILON)
        return wide * inverse, inverse

    def lanes_of(h):
        return pl.ds(pl.multiple_of(h * HEAD_DIM, HEAD_DIM), HEAD_DIM)

    def weights(t, n_all, a, b):
        k = (n_all * b).astype(BF16)
        q = (n_all[WINDOW:] * a).astype(BF16)
        w = jnp.exp(dot(k, q, 1, 1) * SCALE) * masks[t]
        prob = w * (1.0 / jnp.sum(w, axis=0, keepdims=True))
        return q, k, prob

    sum_slot = digit_of(0)

    def backward(j):
        @pl.loop(0, CHUNK_HEADS)
        def _(i):
            lanes = lanes_of(i)
            head = j * CHUNK_HEADS + i
            wide = lanes_of(head)
            a, b, g = (gains[pl.ds(3 + m, 1), wide] for m in range(3))
            x = keys[0, j, :, lanes]
            n_all, inverse = normed(x)
            q, k, prob = weights(0, n_all, a, b)
            p = prob.astype(BF16)
            ct = cot[j, :, lanes].astype(F32)
            d_mix = (ct * g).astype(BF16)
            d_prob = dot(x, d_mix, 1, 1)
            delta = jnp.sum(prob * d_prob, axis=0, keepdims=True)
            d_score = (prob * (d_prob - delta)).astype(BF16)
            mix = dot(p, x, 0, 0)
            d_k = dot(d_score, q, 1, 0)
            d_q = dot(d_score, k, 0, 0)
            d_value = dot(p, d_mix, 1, 0)
            n_own = n_all[WINDOW:]
            d_n = d_k * (b * SCALE)
            d_n_own = d_n[WINDOW:] + d_q * (a * SCALE)

            def through_norm(d, value, scale):
                return scale * (d - value * jnp.mean(d * value, axis=-1, keepdims=True))

            grads[j, :, lanes] = (
                d_value[:WINDOW] + through_norm(d_n[:WINDOW], n_all[:WINDOW], inverse[:WINDOW])
            ).astype(BF16)
            own[j, :, lanes] = d_value[WINDOW:] + through_norm(d_n_own, n_own, inverse[WINDOW:]) + ct
            parts = (
                jnp.sum(d_q * n_own, axis=0, keepdims=True) * SCALE,
                jnp.sum(d_k * n_all, axis=0, keepdims=True) * SCALE,
                jnp.sum(ct * mix, axis=0, keepdims=True),
            )
            for m in range(3):
                sums[0, sum_slot, pl.ds(m * HEADS + head, 1), :] = parts[m]

    def forward(j):
        @pl.loop(0, CHUNK_HEADS)
        def _(i):
            lanes = lanes_of(i)
            wide = lanes_of(j * CHUNK_HEADS + i)
            a, b, g = (gains[pl.ds(m, 1), wide] for m in range(3))
            x = keys[1, j, :, lanes]
            n_all, _ = normed(x)
            _, _, prob = weights(1, n_all, a, b)
            mix = dot(prob.astype(BF16), x, 0, 0)
            produced[j, :, lanes] = (x[WINDOW:].astype(F32) + g * mix).astype(BF16)

    def send_far(j):
        grad_copy(0, j).wait_recv()
        grad_copy(1, j).wait_recv()

        @pl.when(odd == 1)
        def _():
            total = grads[j, rows(slot(4))].astype(F32) + from_partner[1, j].astype(F32)
            grads[j, rows(slot(4))] = total.astype(BF16)

        pl.when(sends_grad[2])(lambda: grad_copy(2, j).start())

    def send_near(j):
        near = grads[j, rows(slot(2))].astype(F32) + from_partner[1 - odd, j].astype(F32)

        @pl.when(gets_grad[2])
        def _():
            grad_copy(2, j).wait_recv()
            grads[j, rows(slot(2))] = (near + from_z4[j].astype(F32)).astype(BF16)

        @pl.when(jnp.logical_not(gets_grad[2]))
        def _():
            grads[j, rows(slot(2))] = near.astype(BF16)

        pl.when(sends_grad[3])(lambda: grad_copy(3, j).start())

    def send_dx(j):
        @pl.when(even)
        def _():
            own[j] = own[j] + from_partner[0, j].astype(F32)

        @pl.when(gets_grad[3])
        def _():
            grad_copy(3, j).wait_recv()
            own[j] = own[j] + from_z2[j].astype(F32)

        dx[j] = own[j].astype(BF16)
        out_copy(1, j).start()

    def middle(j):
        wait_key(0, C, j)
        wait_key(0, D, j)
        load(2, j).wait()
        backward(j)
        grad_copy(0, j).start()
        grad_copy(1, j).start()
        relay(1, j)
        pl.when(j > 0)(lambda: send_far(jnp.maximum(j - 1, 0)))

    each(middle)
    if stages:
        start_sum(0)
    send_far(CHUNKS - 1)
    each(lambda j: relay_last(1, j))
    each(send_near)
    if stages:
        finish_sum(0)

    def last(j):
        wait_key(1, C, j)
        wait_key(1, D, j)
        forward(j)
        out_copy(0, j).start()

    each(last)
    for stage in range(1, len(stages)):
        finish_sum(stage)
    each(send_dx)

    def drain(j):
        for t in range(2):
            for kind in range(4):
                when(sends_key[kind], lambda: key_copy(t, kind, j).wait_send())
        for kind in range(4):
            when(sends_grad[kind], lambda: grad_copy(kind, j).wait_send())
        for kind in range(2):
            out_copy(kind, j).wait_send()
            out_copy(kind, j).wait_recv()

    each(drain)
    for stage, (_, _, factor) in enumerate(stages):
        for offset in range(1, factor):
            sum_copy(stage, offset, digit_of(stage)).wait_send()


def local(
    sizes,
    section_input,
    section_positions,
    saved_input,
    saved_positions,
    cotangent,
    norm_gains,
    output_gains,
    plan,
):
    stages = sum_stages(sizes)
    widest = max([factor for _, _, factor in stages] + [2])
    depth = max(len(stages), 1)
    in_hbm = pl.BlockSpec(memory_space=pl.ANY)
    in_vmem = pl.BlockSpec(memory_space=pltpu.VMEM)
    block = (CHUNKS, TOK, WIDTH)
    produced, grads, totals = pl.pallas_call(
        functools.partial(kernel, sizes),
        out_shape=(
            jax.ShapeDtypeStruct((TOK, FEATURES), BF16),
            jax.ShapeDtypeStruct((TOK, FEATURES), BF16),
            jax.ShapeDtypeStruct((3 * HEADS, HEAD_DIM), F32),
        ),
        in_specs=[
            in_hbm,
            in_vmem,
            in_hbm,
            in_vmem,
            in_hbm,
            in_vmem,
            in_vmem,
            pl.BlockSpec(memory_space=pltpu.SMEM),
        ],
        out_specs=(in_hbm, in_hbm, in_vmem),
        scratch_shapes=[
            pltpu.VMEM((2, CHUNKS, SPAN, WIDTH), BF16),
            pltpu.VMEM(block, BF16),
            pltpu.VMEM((8, FEATURES), F32),
            pltpu.VMEM((2, SPAN, TOK), F32),
            pltpu.VMEM((CHUNKS, WINDOW, WIDTH), BF16),
            pltpu.VMEM(block, F32),
            pltpu.VMEM((2,) + block, BF16),
            pltpu.VMEM(block, BF16),
            pltpu.VMEM(block, BF16),
            pltpu.VMEM(block, BF16),
            pltpu.VMEM(block, BF16),
            pltpu.VMEM((depth, widest, 3 * HEADS, HEAD_DIM), F32),
            pltpu.SemaphoreType.DMA((3, CHUNKS)),
            pltpu.SemaphoreType.DMA((2, 4, CHUNKS)),
            pltpu.SemaphoreType.DMA((2, 4, CHUNKS)),
            pltpu.SemaphoreType.DMA((4, CHUNKS)),
            pltpu.SemaphoreType.DMA((4, CHUNKS)),
            pltpu.SemaphoreType.DMA((2, CHUNKS)),
            pltpu.SemaphoreType.DMA((2, CHUNKS)),
            pltpu.SemaphoreType.DMA((depth, widest)),
            pltpu.SemaphoreType.DMA((depth, widest)),
        ],
        compiler_params=pltpu.CompilerParams(
            collective_id=0, has_side_effects=True, vmem_limit_bytes=40 * 1024 * 1024
        ),
        cost_estimate=pl.CostEstimate(
            flops=9 * 2 * TOK * SPAN * FEATURES,
            bytes_accessed=5 * TOK * FEATURES * 2,
            transcendentals=2 * HEADS * TOK * SPAN,
        ),
    )(
        section_input[0, 0],
        section_positions[0],
        saved_input[0, 0],
        saved_positions[0],
        cotangent[0, 0],
        norm_gains[:, 0],
        output_gains,
        plan[0],
    )
    return (produced[None, None], grads[None, None], totals.reshape(1, 3, FEATURES))


def solution(mesh):
    placed = (
        P("dp", "pipe", "ctx", None),
        P("dp", "pipe", "ctx"),
        P("dp", "pipe", "ctx", None),
        P("dp", "pipe", "ctx"),
        P("dp", "pipe", "ctx", None),
        P(None, "pipe", None, None),
        P(None, "pipe", None),
        P("dp", "pipe", None),
    )
    return jax.shard_map(
        functools.partial(local, {axis: mesh.shape[axis] for axis in ("dp", "pipe", "ctx")}),
        mesh=mesh,
        in_specs=placed,
        out_specs=(
            P("dp", "pipe", "ctx", None),
            P("dp", "pipe", "ctx", None),
            P("pipe", None, None),
        ),
        check_vma=False,
    )
```

time: 322 us -> 106 us (0.33)
  starting transfers between devices: 114 us -> 0 us
  Pallas kernels: 0 us -> 97.3 us
  blocking collectives: 71.7 us -> 0 us
  local copies, waits for them, and re-layouts: 47.1 us -> 7.46 us
  waiting for transfers between devices: 38.8 us -> 0 us
  matrix products: 29.1 us -> 0 us
  other arithmetic: 15.1 us -> 0 us
  between operations: 5.06 us -> 0.67 us
    ppermute x22 -> x0, starting transfers between devices: 114 us -> none  [the longest x20 113 us: passed_along(): lax.ppermute(value, axis, [(source, source + steps) for source in range(f...]
    pallas_call x0 -> x1, Pallas kernels: none -> 97.3 us  [local(): pl.pallas_call(functools.partial(kernel, sizes), out_shape=(jax.ShapeDtyp...]
    psum x1 -> x0, blocking collectives: 71.7 us -> none  [local(): gain_total = lax.psum(gain_grads, ('dp', 'ctx'))]
    ppermute x22 -> x0, waiting for transfers between devices: 38.8 us -> none  [the longest x20 38.8 us: passed_along(): lax.ppermute(value, axis, [(source, source + steps) for source in range(f...]
    dot_general x8 -> x0, matrix products: 29.1 us -> none  [the longest x4 16.3 us: attend(): mixture = jnp.einsum('hqk,khe->qhe', probability, shaped)]
    ppermute x8 -> x0, local copies, waits for them, and re-layouts: 13.2 us -> none  [passed_along(): lax.ppermute(value, axis, [(source, source + steps) for source in range(f...]
    unnamed x33 -> x19, local copies, waits for them, and re-layouts: 17.3 us -> 7.46 us
    reshape x2 -> x0, local copies, waits for them, and re-layouts: 7.54 us -> none  [the longest x1 5.98 us: attend(): shaped = key_rows.reshape(total_rows, HEADS, HEAD_DIM)]
  transfers between devices with their start and end apart: 22 -> 0, of which waited for: 9 -> 0; matrix products, arithmetic and copies ran while one was open for 28% -> 0% of each run, Pallas kernels for 0% -> 0%
where the time goes in v1:
time: 106 us; the launch traced here: 105 us
  Pallas kernels  97.3 us (92%)
  local copies, waits for them, and re-layouts  7.46 us (7%)
    pallas_call x1, Pallas kernels, local(): pl.pallas_call(functools.partial(kernel, sizes), out_shape=(jax.ShapeDtyp...  97.3 us
    unnamed x19, local copies, waits for them, and re-layouts  7.46 us

profile of v1, /device:TPU:0, one launch (start us, length us, event | category | flops | bytes accessed | tf_op | source)
XLA Modules:
  0.0 105.4 jit_solution(7955674156612789289)
XLA Ops:
  0.6 0.0 copy-start.5
  0.6 0.0 copy-start.6
  0.7 0.0 copy-start.7
  0.7 0.6 copy-done.5
  1.3 0.0 copy-done.6
  1.3 0.0 copy-done.7
  1.3 0.0 copy-start
  1.3 1.0 copy-done
  2.4 0.0 copy-start.1
  2.4 1.0 copy-done.1
  3.4 0.0 copy-start.2
  3.4 1.0 copy-done.2
  4.4 0.0 copy-start.3
  4.4 0.8 copy-done.3
  5.2 0.0 copy-start.4
  5.2 0.7 copy-done.4
  5.9 97.3 %shard_map.103 = (bf16[128,2048]{1,0:T(8,128)(2,1)S(1)}, bf16[128,2048]{1,0:T(8,128)(2,1)S(1)}, f32[48,128]{1,0:T(8,128)S(1)}) custom-call(bf16[128,2048]{1,0:T(8,128)(2,1)S(1)} %bitcast.13, s32[1,128]{1,0:T(1,128)S(1)} %bitcast.17, bf16[128,2048]{1,0:T(8,128)(2,1)S(1)} %bitcast.14, s32[1,128]{1,0:T(1,128)S(1)} %bitcast.18, bf16[128,2048]{1,0:T(8,128)(2,1)S(1)} %bitcast.15, ...), custom_call_target="tpu_custom_call" | custom-call | flops 3019898880 | bytes 2621440 | tf_op jit(solution)/shard_map/pallas_call | solution.py:455
  103.2 0.8 copy.16
  104.0 0.8 copy.17
  104.8 0.6 copy.18
Async XLA Ops:
  0.6 0.7 copy-start.5
  0.6 0.7 copy-start.6
  0.7 0.7 copy-start.7
  1.3 1.0 copy-start
  2.4 1.0 copy-start.1
  3.4 1.0 copy-start.2
  4.4 0.8 copy-start.3
  5.2 0.7 copy-start.4

commit v2 on v1

--- a/solution.py
+++ b/solution.py
@@ -23,6 +23,7 @@
 F32 = jnp.float32
 BF16 = jnp.bfloat16
 A, B, C, D = range(4)
+LAST = CHUNKS - 1
 
 
 def sum_stages(sizes):
@@ -67,6 +68,7 @@
     grads,
     own,
     from_partner,
+    from_z3,
     from_z4,
     from_z2,
     produced,
@@ -114,7 +116,8 @@
         elif kind == C:
             source, target, device = jnp.where(even, slot(0), slot(2)), slot(1), partner
         else:
-            source, target, device = jnp.where(even, slot(2), slot(4)), slot(3), partner
+            source = jnp.where(j == LAST, slot(1), jnp.where(even, slot(2), slot(4)))
+            target, device = slot(3), jnp.where(j == LAST, c + 2, partner)
         return pltpu.make_async_remote_copy(
             src_ref=keys.at[t, j, rows(source)],
             dst_ref=keys.at[t, j, rows(target)],
@@ -124,25 +127,26 @@
             device_id_type=MESH,
         )
 
-    sends_key = (up, up & down, even | down, c >= 2 + 2 * odd)
+    def sends_key(kind, j):
+        if kind == D:
+            return ((j == LAST) & up & (c >= 1)) | ((j < LAST) & (c >= 2 + 2 * odd))
+        return (up, up & down, even | down)[kind]
+
     gets_key = (c >= 2, c >= 4, c >= 1, c >= 3)
 
     def grad_copy(kind, j):
-        if kind < 2:
-            source, target, device = slot((1, 3)[kind]), from_partner.at[kind, j], partner
-        else:
-            source, target, device = slot((4, 2)[kind - 2]), (from_z4, from_z2)[kind - 2].at[j], c - 2
+        first = slot((3, 4, 1, 2)[kind])
+        target = (from_z3, from_z4, from_partner, from_z2)[kind].at[j]
         return pltpu.make_async_remote_copy(
-            src_ref=grads.at[j, rows(source)],
+            src_ref=grads.at[j, rows(first)],
             dst_ref=target,
             send_sem=grad_send.at[kind, j],
             recv_sem=grad_recv.at[kind, j],
-            device_id={"ctx": device},
+            device_id={"ctx": partner if kind == 2 else c - 2},
             device_id_type=MESH,
         )
 
-    sends_grad = (None, None, c >= 4, down)
-    gets_grad = (None, None, down & up, up)
+    sends_grad = (down, down, None, down)
 
     def out_copy(kind, j):
         return pltpu.make_async_remote_copy(
@@ -198,13 +202,16 @@
             pl.when(condition)(action)
 
     def start_key(t, kind, j, extra=None):
-        condition = sends_key[kind]
+        condition = sends_key(kind, j)
         if extra is not None:
             condition = condition & extra
         when(condition, lambda: key_copy(t, kind, j).start())
 
-    def wait_key(t, kind, j):
-        when(gets_key[kind], lambda: key_copy(t, kind, j).wait_recv())
+    def wait_key(t, kind, j, extra=None):
+        condition = gets_key[kind]
+        if extra is not None:
+            condition = condition & extra
+        when(condition, lambda: key_copy(t, kind, j).wait_recv())
 
     def each(action):
         @pl.loop(0, CHUNKS)
@@ -267,11 +274,12 @@
         wait_key(t, A, j)
         start_key(t, B, j)
         start_key(t, C, j, odd == 1)
-        start_key(t, D, j, even)
+        start_key(t, D, j, even & (j < LAST))
 
     def relay_last(t, j):
         wait_key(t, B, j)
-        start_key(t, D, j, odd == 1)
+        wait_key(t, C, j, j == LAST)
+        start_key(t, D, j, (odd == 1) | (j == LAST))
 
     each(lambda j: relay(0, j))
 
@@ -351,37 +359,39 @@
             mix = dot(prob.astype(BF16), x, 0, 0)
             produced[j, :, lanes] = (x[WINDOW:].astype(F32) + g * mix).astype(BF16)
 
-    def send_far(j):
-        grad_copy(0, j).wait_recv()
-        grad_copy(1, j).wait_recv()
-
+    def add_to(reach, j, received):
+        total = grads[j, rows(slot(reach))].astype(F32) + received[j].astype(F32)
+        grads[j, rows(slot(reach))] = total.astype(BF16)
+
+    def merge(j):
+        @pl.when(up)
+        def _():
+            grad_copy(0, j).wait_recv()
+            add_to(1, j, from_z3)
+
+        grad_copy(2, j).start()
+
+        @pl.when(up)
+        def _():
+            grad_copy(1, j).wait_recv()
+            add_to(2, j, from_z4)
+
+        pl.when(even & down)(lambda: grad_copy(3, j).start())
+
+    def pass_on(j):
         @pl.when(odd == 1)
         def _():
-            total = grads[j, rows(slot(4))].astype(F32) + from_partner[1, j].astype(F32)
-            grads[j, rows(slot(4))] = total.astype(BF16)
-
-        pl.when(sends_grad[2])(lambda: grad_copy(2, j).start())
-
-    def send_near(j):
-        near = grads[j, rows(slot(2))].astype(F32) + from_partner[1 - odd, j].astype(F32)
-
-        @pl.when(gets_grad[2])
-        def _():
             grad_copy(2, j).wait_recv()
-            grads[j, rows(slot(2))] = (near + from_z4[j].astype(F32)).astype(BF16)
-
-        @pl.when(jnp.logical_not(gets_grad[2]))
-        def _():
-            grads[j, rows(slot(2))] = near.astype(BF16)
-
-        pl.when(sends_grad[3])(lambda: grad_copy(3, j).start())
+            add_to(2, j, from_partner)
+            pl.when(down)(lambda: grad_copy(3, j).start())
 
     def send_dx(j):
         @pl.when(even)
         def _():
-            own[j] = own[j] + from_partner[0, j].astype(F32)
-
-        @pl.when(gets_grad[3])
+            grad_copy(2, j).wait_recv()
+            own[j] = own[j] + from_partner[j].astype(F32)
+
+        @pl.when(up)
         def _():
             grad_copy(3, j).wait_recv()
             own[j] = own[j] + from_z2[j].astype(F32)
@@ -390,39 +400,45 @@
         out_copy(1, j).start()
 
     def middle(j):
-        wait_key(0, C, j)
+        wait_key(0, C, j, j < LAST)
         wait_key(0, D, j)
-        load(2, j).wait()
+        pl.when(j == 0)(lambda: each(lambda i: load(2, i).wait()))
         backward(j)
-        grad_copy(0, j).start()
-        grad_copy(1, j).start()
+        for kind in range(2):
+            when(sends_grad[kind], lambda: grad_copy(kind, j).start())
         relay(1, j)
-        pl.when(j > 0)(lambda: send_far(jnp.maximum(j - 1, 0)))
+        pl.when(j > 0)(lambda: merge(jnp.maximum(j - 1, 0)))
 
     each(middle)
     if stages:
         start_sum(0)
-    send_far(CHUNKS - 1)
-    each(lambda j: relay_last(1, j))
-    each(send_near)
+    merge(LAST)
+
+    def between(j):
+        pass_on(j)
+        relay_last(1, j)
+
+    each(between)
     if stages:
         finish_sum(0)
 
     def last(j):
-        wait_key(1, C, j)
+        wait_key(1, C, j, j < LAST)
         wait_key(1, D, j)
         forward(j)
         out_copy(0, j).start()
+        for stage in range(1, min(CHUNKS + 1, len(stages))):
+            pl.when(j == stage - 1)(lambda: finish_sum(stage))
+        send_dx(j)
 
     each(last)
-    for stage in range(1, len(stages)):
+    for stage in range(CHUNKS + 1, len(stages)):
         finish_sum(stage)
-    each(send_dx)
 
     def drain(j):
         for t in range(2):
             for kind in range(4):
-                when(sends_key[kind], lambda: key_copy(t, kind, j).wait_send())
+                when(sends_key(kind, j), lambda: key_copy(t, kind, j).wait_send())
         for kind in range(4):
             when(sends_grad[kind], lambda: grad_copy(kind, j).wait_send())
         for kind in range(2):
@@ -477,7 +493,8 @@
             pltpu.VMEM((2, SPAN, TOK), F32),
             pltpu.VMEM((CHUNKS, WINDOW, WIDTH), BF16),
             pltpu.VMEM(block, F32),
-            pltpu.VMEM((2,) + block, BF16),
+            pltpu.VMEM(block, BF16),
+            pltpu.VMEM(block, BF16),
             pltpu.VMEM(block, BF16),
             pltpu.VMEM(block, BF16),
             pltpu.VMEM(block, BF16),
@@ -494,7 +511,7 @@
             pltpu.SemaphoreType.DMA((depth, widest)),
         ],
         compiler_params=pltpu.CompilerParams(
-            collective_id=0, has_side_effects=True, vmem_limit_bytes=40 * 1024 * 1024
+            collective_id=0, has_side_effects=True, vmem_limit_bytes=60 * 1024 * 1024
         ),
         cost_estimate=pl.CostEstimate(
             flops=9 * 2 * TOK * SPAN * FEATURES,

time: 106 us -> 83.6 us (0.79)
  Pallas kernels: 97.3 us -> 79.4 us
  local copies, waits for them, and re-layouts: 7.46 us -> 3.35 us
    pallas_call x1, Pallas kernels: 97.3 us -> 79.4 us  [local(): pl.pallas_call(functools.partial(kernel, sizes), out_shape=(jax.ShapeDtyp...]
    unnamed x19 -> x7, local copies, waits for them, and re-layouts: 7.46 us -> 3.35 us
where the time goes in v2:
time: 83.6 us; the launch traced here: 83.4 us
  Pallas kernels  79.4 us (95%)
  local copies, waits for them, and re-layouts  3.35 us (4%)
    pallas_call x1, Pallas kernels, local(): pl.pallas_call(functools.partial(kernel, sizes), out_shape=(jax.ShapeDtyp...  79.4 us
    unnamed x7, local copies, waits for them, and re-layouts  3.35 us

profile of v2, /device:TPU:0, one launch (start us, length us, event | category | flops | bytes accessed | tf_op | source)
XLA Modules:
  0.0 83.4 jit_solution(11526002950455894851)
XLA Ops:
  0.6 79.4 %shard_map.103 = (bf16[128,2048]{1,0:T(8,128)(2,1)}, bf16[128,2048]{1,0:T(8,128)(2,1)}, f32[48,128]{1,0:T(8,128)}) custom-call(bf16[128,2048]{1,0:T(8,128)(2,1)} %bitcast.13, s32[1,128]{1,0:T(1,128)} %bitcast.17, bf16[128,2048]{1,0:T(8,128)(2,1)} %bitcast.14, s32[1,128]{1,0:T(1,128)} %bitcast.18, bf16[128,2048]{1,0:T(8,128)(2,1)} %bitcast.15, ...), custom_call_target="tpu_custom_call" | custom-call | flops 3019898880 | bytes 2621440 | tf_op jit(solution)/shard_map/pallas_call | solution.py:471
  80.0 0.0 copy-start
  80.0 1.9 %copy.16 = bf16[1,1,128,2048]{3,2,1,0:T(8,128)(2,1)} copy(bf16[1,1,128,2048]{3,2,1,0:T(8,128)(2,1)} %bitcast.11) | data formatting | bytes 1048576
  82.0 0.0 copy-done
  82.0 0.0 copy-start.1
  82.0 0.8 copy.17
  82.8 0.0 copy-done.1
  82.8 0.6 copy.18
Async XLA Ops:
  80.0 2.0 %copy-start = (bf16[128,2048]{1,0:T(8,128)(2,1)S(1)}, bf16[128,2048]{1,0:T(8,128)(2,1)}, u32[]{:S(2)}) copy-start(bf16[128,2048]{1,0:T(8,128)(2,1)} %get-tuple-element.7) | copy-start | bytes 1572868
  82.0 0.8 copy-start.1

commit v3 on v2

--- a/solution.py
+++ b/solution.py
@@ -309,7 +309,7 @@
     sum_slot = digit_of(0)
 
     def backward(j):
-        @pl.loop(0, CHUNK_HEADS)
+        @pl.loop(0, CHUNK_HEADS, unroll=4)
         def _(i):
             lanes = lanes_of(i)
             head = j * CHUNK_HEADS + i
@@ -348,7 +348,7 @@
                 sums[0, sum_slot, pl.ds(m * HEADS + head, 1), :] = parts[m]
 
     def forward(j):
-        @pl.loop(0, CHUNK_HEADS)
+        @pl.loop(0, CHUNK_HEADS, unroll=4)
         def _(i):
             lanes = lanes_of(i)
             wide = lanes_of(j * CHUNK_HEADS + i)

time: 83.6 us -> 80.8 us (0.967)
  Pallas kernels: 79.4 us -> 76.4 us
    pallas_call x1, Pallas kernels: 79.4 us -> 76.4 us  [local(): pl.pallas_call(functools.partial(kernel, sizes), out_shape=(jax.ShapeDtyp...]
where the time goes in v3:
time: 80.8 us; the launch traced here: 80.4 us
  Pallas kernels  76.4 us (95%)
  local copies, waits for them, and re-layouts  3.35 us (4%)
    pallas_call x1, Pallas kernels, local(): pl.pallas_call(functools.partial(kernel, sizes), out_shape=(jax.ShapeDtyp...  76.4 us
    unnamed x7, local copies, waits for them, and re-layouts  3.35 us

profile of v3, /device:TPU:0, one launch (start us, length us, event | category | flops | bytes accessed | tf_op | source)
XLA Modules:
  0.0 80.4 jit_solution(746290577605197269)
XLA Ops:
  0.6 76.4 %shard_map.103 = (bf16[128,2048]{1,0:T(8,128)(2,1)}, bf16[128,2048]{1,0:T(8,128)(2,1)}, f32[48,128]{1,0:T(8,128)}) custom-call(bf16[128,2048]{1,0:T(8,128)(2,1)} %bitcast.13, s32[1,128]{1,0:T(1,128)} %bitcast.17, bf16[128,2048]{1,0:T(8,128)(2,1)} %bitcast.14, s32[1,128]{1,0:T(1,128)} %bitcast.18, bf16[128,2048]{1,0:T(8,128)(2,1)} %bitcast.15, ...), custom_call_target="tpu_custom_call" | custom-call | flops 3019898880 | bytes 2621440 | tf_op jit(solution)/shard_map/pallas_call | solution.py:471
  77.1 0.0 copy-start
  77.1 1.9 %copy.16 = bf16[1,1,128,2048]{3,2,1,0:T(8,128)(2,1)} copy(bf16[1,1,128,2048]{3,2,1,0:T(8,128)(2,1)} %bitcast.11) | data formatting | bytes 1048576
  79.0 0.0 copy-done
  79.0 0.0 copy-start.1
  79.0 0.8 copy.17
  79.8 0.0 copy-done.1
  79.8 0.6 copy.18
Async XLA Ops:
  77.1 2.0 %copy-start = (bf16[128,2048]{1,0:T(8,128)(2,1)S(1)}, bf16[128,2048]{1,0:T(8,128)(2,1)}, u32[]{:S(2)}) copy-start(bf16[128,2048]{1,0:T(8,128)(2,1)} %get-tuple-element.7) | copy-start | bytes 1572868
  79.0 0.8 copy-start.1
